TPU v7x, 32 devices: a whole 2x2x4 slice. The times are simulated.
32 devices in a mesh: samp: 4 (over y, x), ind: 8 (over z, core).
Axes of the slice: x: 2, y: 2, z: 4, core: 2. Of those that a mesh axis runs over, the one named last changes fastest.
Arguments:
- points: bfloat16 [8192, 64], P('samp'), may hold values from -6 to 6
- centers: bfloat16 [65536, 64], P('ind'), may hold values from -6 to 6
- coeffs: bfloat16 [65536, 128], P('ind'), may hold values from -0.6 to 0.6
- targets: bfloat16 [8192, 128], P('samp'), may hold values from 0 to 1
- diag_inv: float32 [128, 512, 512], P('ind'), may hold values from -3 to 15
- low_left: bfloat16 [128, 512, 64], P('ind'), may hold values from -0.0014648438 to 0.0014648438
- low_right: bfloat16 [128, 512, 64], P('ind'), may hold values from -0.25 to 0.25
- decay_rates: float32 [128, 64], P('ind'), may hold values from 0.05 to 64
- block_ranks: int32 [128], P('ind'), may hold values from 16 to 64
Outputs:
- direction: float32 [65536, 128], P('ind')
All inputs are finite; a program needn't handle non-finite values.
Results may differ from a plain program's by a relative error of at most 0.0003.
Values may be sent and summed in bfloat16 or wider, within the bound.
A program may use at most 128 MiB of HBM per device.

v0:
```python
import math

import jax
import jax.numpy as jnp
from jax import lax
from jax.sharding import PartitionSpec as P

D = 64
B = 512
R = 64
NB = 128


highest = lax.Precision.HIGHEST
ridge_weight = 0.1


def from_behind(block, axis, distance):
    devices = range(lax.axis_size(axis))
    route = [(i - distance, i) for i in devices if i - distance in devices]
    return lax.ppermute(block, axis, route)


def kernel_tile(points, point_sq, center_block):
    center_sq = jnp.sum(jnp.square(center_block.astype(jnp.float32)), axis=1)
    cross_term = lax.dot_general(
        points, center_block, (((1,), (1,)), ((), ())), preferred_element_type=jnp.float32
    )
    distance = point_sq[:, None] + center_sq[None, :] - 2.0 * cross_term
    return jnp.exp(-(1.0 / D) * distance).astype(jnp.bfloat16)


def solve_step(state, inputs):
    inv_block, left_block, right_block, decay_block, grad_block = inputs
    rhs_block = grad_block - jnp.dot(left_block, state, precision=highest)
    solved = jnp.dot(inv_block, rhs_block, precision=highest)
    state = decay_block[:, None] * state + jnp.dot(right_block.T, solved, precision=highest)
    return (state, solved)


def summarize(carried, inputs):
    transfer, offset = carried
    inv_block, left_block, right_block, decay_block, grad_block = inputs
    projected = jnp.dot(right_block.T, inv_block, precision=highest)
    step_map = jnp.diag(decay_block) - jnp.dot(projected, left_block, precision=highest)
    transfer = jnp.dot(step_map, transfer, precision=highest)
    offset = jnp.dot(step_map, offset, precision=highest) + jnp.dot(
        projected, grad_block, precision=highest
    )
    return ((transfer, offset), None)


def body(points, centers, coeffs, targets, diag_inv, low_left, low_right, decay_rates, block_ranks):
    sample_rows = points.shape[0]
    inducing_rows = centers.shape[0]
    label_count = coeffs.shape[1]
    block_width = 2 * B
    block_count = inducing_rows // block_width
    center_blocks = centers.reshape(block_count, block_width, D)
    coeff_blocks = coeffs.reshape(block_count, block_width, label_count)
    point_sq = jnp.sum(jnp.square(points.astype(jnp.float32)), axis=1)

    def predict_step(running, paired):
        kernel_part = kernel_tile(points, point_sq, paired[0])
        running = running + jnp.dot(kernel_part, paired[1], preferred_element_type=jnp.float32)
        return (running, kernel_part)

    partial_value, stored = lax.scan(
        predict_step,
        jnp.zeros((sample_rows, label_count), jnp.float32),
        (center_blocks, coeff_blocks),
    )
    pred_part = lax.psum_scatter(partial_value, "ind", scatter_dimension=0, tiled=True)
    share_rows = pred_part.shape[0]
    own_targets = lax.dynamic_slice_in_dim(
        targets, lax.axis_index("ind") * share_rows, share_rows, 0
    )
    resid_part = (jax.nn.sigmoid(pred_part) - own_targets.astype(jnp.float32)).astype(jnp.bfloat16)
    residual = lax.all_gather(resid_part, "ind", axis=0, tiled=True)

    def gradient_piece(kernel_part):
        return lax.dot_general(
            kernel_part, residual, (((0,), (0,)), ((), ())), preferred_element_type=jnp.float32
        )

    pieces = lax.map(gradient_piece, stored).reshape(inducing_rows, label_count)
    scaling = 1.0 / math.sqrt(sample_rows * lax.axis_size("samp"))
    summed = lax.psum(pieces, "samp")
    gradient = summed * scaling + ridge_weight * coeffs.astype(jnp.float32)
    local_blocks = inducing_rows // B
    rank_mask = (jnp.arange(R)[None, :] < block_ranks[:, None]).astype(jnp.float32)
    left_masked = low_left.astype(jnp.float32) * rank_mask[:, None, :]
    right_masked = low_right.astype(jnp.float32) * rank_mask[:, None, :]
    decays = jnp.exp(-decay_rates / NB)
    grad_blocks = gradient.reshape(local_blocks, B, label_count)
    inputs = (diag_inv, left_masked, right_masked, decays, grad_blocks)
    identity_map = jnp.eye(R, dtype=jnp.float32)
    empty_state = jnp.zeros((R, label_count), jnp.float32)
    (transfer, offset), _ = lax.scan(summarize, (identity_map, empty_state), inputs)

    def relay_step(turn_index, carried):
        moved = jnp.dot(transfer, carried, precision=highest) + offset
        return from_behind(moved.astype(jnp.bfloat16), "ind", 1).astype(moved.dtype)

    entering = lax.fori_loop(0, lax.axis_size("ind") - 1, relay_step, empty_state)
    _, solved = lax.scan(solve_step, entering, inputs)
    direction = solved.reshape(inducing_rows, label_count)
    return direction


def solution(mesh):
    return jax.shard_map(
        body,
        mesh=mesh,
        in_specs=(
            P("samp", None),
            P("ind", None),
            P("ind", None),
            P("samp", None),
            P("ind", None, None),
            P("ind", None, None),
            P("ind", None, None),
            P("ind", None),
            P("ind"),
        ),
        out_specs=P("ind", None),
        check_vma=False,
    )
```

profile of v0, /device:TPU:0, one launch (start us, length us, event | category | flops | bytes accessed | tf_op | source)
XLA Modules:
  0.0 491.6 jit_solution(2801782260752353698)
XLA Ops:
  9.6 75.1 %while.61 = (s32[]{:T(128)}, f32[2048,128]{1,0:T(8,128)S(1)}, bf16[8,2048,1024]{1,2,0:T(8,128)(2,1)}, f32[2048]{0:T(1024)S(1)}, bf16[8,1024,64]{2,1,0:T(8,128)(2...) while((s32[]{:T(128)}, f32[2048,128]{1,0:T(8,128)S(1)}, ...), condition=%wide.region_3.4_spmd.clone, body=%wide.region_1.3_spmd.clone.sunk | while | flops 816512000 | bytes 15615595 | solution.py:68
  9.8 5.4 %bitcast_dynamic-update-slice_fusion.5 = (bf16[8,2048,1024]{1,2,0:T(8,128)(2,1)}, bf16[2048,1024]{0,1:T(8,128)(2,1)}) fusion(bf16[8,2048,1024]{1,2,0:T(8,128)(2,1)} %get-tuple-element.527, s32[]{:T(128)} %get-tuple-element.525, bf16[2048,64]{0,1:T(8,128)(2,1)} %get-tuple-element.539, bf16[8,1024,64]{2,1,0:T(8,128)(2,1)S(1)} %get-tuple-element.538, ...), kind=kOutput, calls=%fused_computation.25.clone.1 | convolution fusion | flops 278921216 | bytes 8926208 | tf_op jit(solution)/shard_map/while/body/eval_jaxpr/dot_general | solution.py:26
  15.2 3.7 convolution_add_fusion.8
  19.2 5.5 %bitcast_dynamic-update-slice_fusion.5 = (bf16[8,2048,1024]{1,2,0:T(8,128)(2,1)}, bf16[2048,1024]{0,1:T(8,128)(2,1)}) fusion(bf16[8,2048,1024]{1,2,0:T(8,128)(2,1)} %get-tuple-element.527, s32[]{:T(128)} %get-tuple-element.525, bf16[2048,64]{0,1:T(8,128)(2,1)} %get-tuple-element.539, bf16[8,1024,64]{2,1,0:T(8,128)(2,1)S(1)} %get-tuple-element.538, ...), kind=kOutput, calls=%fused_computation.25.clone.1 | convolution fusion | flops 278921216 | bytes 8926208 | tf_op jit(solution)/shard_map/while/body/eval_jaxpr/dot_general | solution.py:26
  24.6 3.7 convolution_add_fusion.8
  28.6 5.4 %bitcast_dynamic-update-slice_fusion.5 = (bf16[8,2048,1024]{1,2,0:T(8,128)(2,1)}, bf16[2048,1024]{0,1:T(8,128)(2,1)}) fusion(bf16[8,2048,1024]{1,2,0:T(8,128)(2,1)} %get-tuple-element.527, s32[]{:T(128)} %get-tuple-element.525, bf16[2048,64]{0,1:T(8,128)(2,1)} %get-tuple-element.539, bf16[8,1024,64]{2,1,0:T(8,128)(2,1)S(1)} %get-tuple-element.538, ...), kind=kOutput, calls=%fused_computation.25.clone.1 | convolution fusion | flops 278921216 | bytes 8926208 | tf_op jit(solution)/shard_map/while/body/eval_jaxpr/dot_general | solution.py:26
  34.0 3.7 convolution_add_fusion.8
  38.0 5.4 %bitcast_dynamic-update-slice_fusion.5 = (bf16[8,2048,1024]{1,2,0:T(8,128)(2,1)}, bf16[2048,1024]{0,1:T(8,128)(2,1)}) fusion(bf16[8,2048,1024]{1,2,0:T(8,128)(2,1)} %get-tuple-element.527, s32[]{:T(128)} %get-tuple-element.525, bf16[2048,64]{0,1:T(8,128)(2,1)} %get-tuple-element.539, bf16[8,1024,64]{2,1,0:T(8,128)(2,1)S(1)} %get-tuple-element.538, ...), kind=kOutput, calls=%fused_computation.25.clone.1 | convolution fusion | flops 278921216 | bytes 8926208 | tf_op jit(solution)/shard_map/while/body/eval_jaxpr/dot_general | solution.py:26
  43.4 3.7 convolution_add_fusion.8
  47.4 5.4 %bitcast_dynamic-update-slice_fusion.5 = (bf16[8,2048,1024]{1,2,0:T(8,128)(2,1)}, bf16[2048,1024]{0,1:T(8,128)(2,1)}) fusion(bf16[8,2048,1024]{1,2,0:T(8,128)(2,1)} %get-tuple-element.527, s32[]{:T(128)} %get-tuple-element.525, bf16[2048,64]{0,1:T(8,128)(2,1)} %get-tuple-element.539, bf16[8,1024,64]{2,1,0:T(8,128)(2,1)S(1)} %get-tuple-element.538, ...), kind=kOutput, calls=%fused_computation.25.clone.1 | convolution fusion | flops 278921216 | bytes 8926208 | tf_op jit(solution)/shard_map/while/body/eval_jaxpr/dot_general | solution.py:26
  52.8 3.7 convolution_add_fusion.8
  56.7 5.5 %bitcast_dynamic-update-slice_fusion.5 = (bf16[8,2048,1024]{1,2,0:T(8,128)(2,1)}, bf16[2048,1024]{0,1:T(8,128)(2,1)}) fusion(bf16[8,2048,1024]{1,2,0:T(8,128)(2,1)} %get-tuple-element.527, s32[]{:T(128)} %get-tuple-element.525, bf16[2048,64]{0,1:T(8,128)(2,1)} %get-tuple-element.539, bf16[8,1024,64]{2,1,0:T(8,128)(2,1)S(1)} %get-tuple-element.538, ...), kind=kOutput, calls=%fused_computation.25.clone.1 | convolution fusion | flops 278921216 | bytes 8926208 | tf_op jit(solution)/shard_map/while/body/eval_jaxpr/dot_general | solution.py:26
  62.2 3.7 convolution_add_fusion.8
  66.2 5.4 %bitcast_dynamic-update-slice_fusion.5 = (bf16[8,2048,1024]{1,2,0:T(8,128)(2,1)}, bf16[2048,1024]{0,1:T(8,128)(2,1)}) fusion(bf16[8,2048,1024]{1,2,0:T(8,128)(2,1)} %get-tuple-element.527, s32[]{:T(128)} %get-tuple-element.525, bf16[2048,64]{0,1:T(8,128)(2,1)} %get-tuple-element.539, bf16[8,1024,64]{2,1,0:T(8,128)(2,1)S(1)} %get-tuple-element.538, ...), kind=kOutput, calls=%fused_computation.25.clone.1 | convolution fusion | flops 278921216 | bytes 8926208 | tf_op jit(solution)/shard_map/while/body/eval_jaxpr/dot_general | solution.py:26
  71.6 3.7 convolution_add_fusion.8
  75.6 5.4 %bitcast_dynamic-update-slice_fusion.5 = (bf16[8,2048,1024]{1,2,0:T(8,128)(2,1)}, bf16[2048,1024]{0,1:T(8,128)(2,1)}) fusion(bf16[8,2048,1024]{1,2,0:T(8,128)(2,1)} %get-tuple-element.527, s32[]{:T(128)} %get-tuple-element.525, bf16[2048,64]{0,1:T(8,128)(2,1)} %get-tuple-element.539, bf16[8,1024,64]{2,1,0:T(8,128)(2,1)S(1)} %get-tuple-element.538, ...), kind=kOutput, calls=%fused_computation.25.clone.1 | convolution fusion | flops 278921216 | bytes 8926208 | tf_op jit(solution)/shard_map/while/body/eval_jaxpr/dot_general | solution.py:26
  81.0 3.7 convolution_add_fusion.8
  85.8 35.1 %reduce-scatter.2.cloned.1.call-done = f32[256,128]{1,0:T(8,128)} async-done(((f32[2048,128]{1,0:T(8,128)}), f32[256,128]{1,0:T(8,128)}) %reduce-scatter.2.cloned.1.call-update) | async-done | bytes 131088 | tf_op jit(solution)/shard_map/reduce_scatter | solution.py:73
  121.8 15.0 %all_gather.3 = bf16[2048,128]{1,0:T(8,128)(2,1)S(1)} all-gather(bf16[256,128]{1,0:T(8,128)(2,1)S(1)} %subtract_convert_fusion), channel_id=1, replica_groups=mesh['samp'=4,'ind'=8] {'ind'}, dimensions={0}, use_global_device_ids=true | all-gather | bytes 589824 | tf_op jit(solution)/shard_map/all_gather | solution.py:79
  136.8 33.9 %while.59 = (s32[]{:T(128)}, f32[8,1024,128]{2,1,0:T(8,128)}, bf16[8,2048,1024]{1,2,0:T(8,128)(2,1)}, bf16[2048,128]{1,0:T(8,128)(2,1)S(1)}, s32[]{:T(128)}) while((s32[]{:T(128)}, f32[8,1024,128]{2,1,0:T(8,128)}, bf16[8,2048,1024]{1,2,0:T(8,128)(2,1)}, bf16[2048,128]{1,0:T(8,128)(2,1)S(1)}, s32[]{:T(128)}) %tuple.93), condition=%wide.region_6.7_spmd, body=%wide.region_5.6_spmd.sunk | while | flops 536870912 | bytes 5243965 | solution.py:86
  136.8 4.2 fusion.99
  141.1 4.3 fusion.99
  145.3 4.3 fusion.99
  149.6 4.2 fusion.99
  153.8 4.2 fusion.99
  158.1 4.2 fusion.99
  162.3 4.2 fusion.99
  166.5 4.2 fusion.99
  175.9 5.9 %convert_multiply_fusion = (f32[16,512,64]{2,1,0:T(8,128)}, f32[16,512,64]{2,1,0:T(8,128)}) fusion(bf16[16,512,64]{2,1,0:T(8,128)(2,1)} %copy.11, f32[16,64]{1,0:T(8,128)S(1)} %fusion.54, bf16[16,512,64]{2,1,0:T(8,128)(2,1)S(1)} %copy.10), kind=kLoop, calls=%fused_computation.63 | loop fusion | flops 2097152 | bytes 6295552 | tf_op jit(solution)/shard_map/mul | solution.py:92
  181.8 91.3 %all-reduce.2.cloned.1.call-done = f32[8192,128]{1,0:T(8,128)} async-done(((f32[8192,128]{1,0:T(8,128)}), f32[8192,128]{1,0:T(8,128)}) %all-reduce.2.cloned.1.call-update) | async-done | bytes 4194320 | tf_op jit(solution)/shard_map/psum | solution.py:88
  273.1 5.4 %multiply_add_fusion = f32[8192,128]{1,0:T(8,128)} fusion(bf16[8192,128]{1,0:T(8,128)(2,1)} %bitcast.139, f32[8192,128]{1,0:T(8,128)} %all-reduce.2.cloned.1.call-done), kind=kLoop, calls=%fused_computation.62 | loop fusion | flops 4194304 | bytes 10485760 | tf_op jit(solution)/shard_map/add | solution.py:89
  278.5 78.5 %while.62 = (s32[]{:T(128)}, f32[64,64]{1,0:T(8,128)S(1)}, f32[64,128]{1,0:T(8,128)S(1)}, f32[16,64]{1,0:T(8,128)S(1)}, f32[16,512,64]{2,1,0:T(8,128)}, /*index=...) while((s32[]{:T(128)}, f32[64,64]{1,0:T(8,128)S(1)}, ...), condition=%wide.region_9.10_spmd.clone, body=%wide.region_8.9_spmd.clone.sunk | while | flops 286289920 | bytes 2542451 | solution.py:99
  357.0 33.7 %while.63 = (s32[]{:T(128)}, f32[64,128]{1,0:T(8,128)S(1)}, f32[64,64]{1,0:T(8,128)S(1)}, f32[64,128]{1,0:T(8,128)S(1)}, s32[]{:T(128)}, /*index=5*/s32[]{:T(128)}) while((s32[]{:T(128)}, f32[64,128]{1,0:T(8,128)S(1)}, f32[64,64]{1,0:T(8,128)S(1)}, f32[64,128]{1,0:T(8,128)S(1)}, s32[]{:T(128)}, /*index=5*/s32[]{:T(128)}) %tuple.99), condition=%wide.region_11.12_spmd.clone, body=%wide.region_10.11_spmd.clone.sunk | while | flops 6324227 | bytes 213111 | solution.py:105
  360.0 3.7 collective-permute-start
  364.7 4.2 collective-permute-start
  369.9 4.2 collective-permute-start
  375.1 4.2 collective-permute-start
  380.4 4.2 collective-permute-start
  385.6 4.2 collective-permute-start
  390.7 94.0 %while.60 = (s32[]{:T(128)}, f32[64,128]{1,0:T(8,128)S(1)}, f32[16,512,128]{2,1,0:T(8,128)}, f32[16,64]{1,0:T(8,128)S(1)}, f32[16,512,64]{2,1,0:T(8,128)}, /*ind...) while((s32[]{:T(128)}, f32[64,128]{1,0:T(8,128)S(1)}, ...), condition=%wide.region_13.14_spmd, body=%wide.region_12.13_spmd.sunk | while | flops 503398400 | bytes 3247457 | solution.py:106
  392.1 2.9 bitcast_dynamic-update-slice_fusion.4
  397.9 2.9 bitcast_dynamic-update-slice_fusion.4
  403.8 2.9 bitcast_dynamic-update-slice_fusion.4
  409.7 2.9 bitcast_dynamic-update-slice_fusion.4
  415.6 2.9 bitcast_dynamic-update-slice_fusion.4
  421.5 2.9 bitcast_dynamic-update-slice_fusion.4
  433.2 2.9 bitcast_dynamic-update-slice_fusion.4
  439.1 2.9 bitcast_dynamic-update-slice_fusion.4
  (240 shorter events, 168.1 us)
Async XLA Ops:
  6.5 114.3 %reduce-scatter.2.cloned.1.call-start = ((), (), s32[]{:S(2)}) async-start(), calls=%async_computation.1 | async-start | bytes 1179648 | tf_op jit(solution)/shard_map/reduce_scatter | solution.py:73
  84.7 1.0 copy-start
  85.7 187.4 %all-reduce.2.cloned.1.call-start = ((), (), s32[]{:S(2)}) async-start(), calls=%async_computation.2 | async-start | bytes 8388608 | tf_op jit(solution)/shard_map/psum | solution.py:88
  170.8 1.2 copy-start.1
  170.8 5.0 %copy-start.3 = (s32[16]{0:T(128)S(1)}, s32[16]{0:T(128)}, u32[]{:S(2)}) copy-start(s32[16]{0:T(128)} %param.27) | copy-start | bytes 196
  170.8 5.1 %copy-start.2 = (f32[16,64]{1,0:T(8,128)S(1)}, f32[16,64]{1,0:T(8,128)}, u32[]{:S(2)}) copy-start(f32[16,64]{1,0:T(8,128)} %param.26) | copy-start | bytes 12292
  357.2 2.6 collective-permute-start
  360.0 4.5 collective-permute-start
  364.7 5.1 %collective-permute-start = (bf16[64,128]{1,0:T(8,128)(2,1)S(1)}, bf16[64,128]{1,0:T(8,128)(2,1)S(1)}, u32[]{:S(2)}, u32[]{:S(2)}) collective-permute-start(bf16[64,128]{1,0:T(8,128)(2,1)S(1)} %fusion.125), channel_id=1, source_target_pairs={{0,1},{1,2},{2,3},{3,4},{4,5},{5,6},{6,7},{8,9},{9,10},{10,11},{11... | collective-permute-start | bytes 49160 | tf_op jit(solution)/shard_map/while/body/eval_jaxpr/ppermute | solution.py:21
  369.9 5.1 %collective-permute-start = (bf16[64,128]{1,0:T(8,128)(2,1)S(1)}, bf16[64,128]{1,0:T(8,128)(2,1)S(1)}, u32[]{:S(2)}, u32[]{:S(2)}) collective-permute-start(bf16[64,128]{1,0:T(8,128)(2,1)S(1)} %fusion.125), channel_id=1, source_target_pairs={{0,1},{1,2},{2,3},{3,4},{4,5},{5,6},{6,7},{8,9},{9,10},{10,11},{11... | collective-permute-start | bytes 49160 | tf_op jit(solution)/shard_map/while/body/eval_jaxpr/ppermute | solution.py:21
  375.1 5.1 %collective-permute-start = (bf16[64,128]{1,0:T(8,128)(2,1)S(1)}, bf16[64,128]{1,0:T(8,128)(2,1)S(1)}, u32[]{:S(2)}, u32[]{:S(2)}) collective-permute-start(bf16[64,128]{1,0:T(8,128)(2,1)S(1)} %fusion.125), channel_id=1, source_target_pairs={{0,1},{1,2},{2,3},{3,4},{4,5},{5,6},{6,7},{8,9},{9,10},{10,11},{11... | collective-permute-start | bytes 49160 | tf_op jit(solution)/shard_map/while/body/eval_jaxpr/ppermute | solution.py:21
  380.4 5.1 %collective-permute-start = (bf16[64,128]{1,0:T(8,128)(2,1)S(1)}, bf16[64,128]{1,0:T(8,128)(2,1)S(1)}, u32[]{:S(2)}, u32[]{:S(2)}) collective-permute-start(bf16[64,128]{1,0:T(8,128)(2,1)S(1)} %fusion.125), channel_id=1, source_target_pairs={{0,1},{1,2},{2,3},{3,4},{4,5},{5,6},{6,7},{8,9},{9,10},{10,11},{11... | collective-permute-start | bytes 49160 | tf_op jit(solution)/shard_map/while/body/eval_jaxpr/ppermute | solution.py:21
  385.6 5.1 %collective-permute-start = (bf16[64,128]{1,0:T(8,128)(2,1)S(1)}, bf16[64,128]{1,0:T(8,128)(2,1)S(1)}, u32[]{:S(2)}, u32[]{:S(2)}) collective-permute-start(bf16[64,128]{1,0:T(8,128)(2,1)S(1)} %fusion.125), channel_id=1, source_target_pairs={{0,1},{1,2},{2,3},{3,4},{4,5},{5,6},{6,7},{8,9},{9,10},{10,11},{11... | collective-permute-start | bytes 49160 | tf_op jit(solution)/shard_map/while/body/eval_jaxpr/ppermute | solution.py:21
Sparse Core Ops, SparseCore 0:
  85.8 35.0 reduce-scatter.1
  170.9 102.1 all-reduce.1
where the time goes:
time: 497 us; the launch traced here: 492 us
  matrix products  279 us (56%)
  waiting for transfers between devices  132 us (27%)
  starting transfers between devices  26.6 us (5%)
  other arithmetic  15.1 us (3%)
  blocking collectives  15 us (3%)
  between operations  13.5 us (3%)
  local copies, waits for them, and re-layouts  8.32 us (2%)
    psum x1, waiting for transfers between devices, body(): summed = lax.psum(pieces, 'samp')  91.3 us
    dot_general x16, matrix products, solve_step(): solved = jnp.dot(inv_block, rhs_block, precision=highest)  46.7 us
    dot_general x8, matrix products, kernel_tile(): lax.dot_general(points, center_block, (((1,), (1,)), ((), ())), preferred...  43.4 us
    reduce_scatter x1, waiting for transfers between devices, body(): lax.psum_scatter(partial_value, 'ind', scatter_dimension=0, tiled=True)  35.1 us
    dot_general x8, matrix products, gradient_piece(): lax.dot_general(kernel_part, residual, (((0,), (0,)), ((), ())), preferre...  33.9 us
    dot_general x16, matrix products, summarize(): projected = jnp.dot(right_block.T, inv_block, precision=highest)  32.4 us
    dot_general x8, matrix products, predict_step(): jnp.dot(kernel_part, paired[1], preferred_element_type=jnp.float32)  29.8 us
    ppermute x7, starting transfers between devices, from_behind(): return lax.ppermute(block, axis, route)  26.6 us
  transfers between devices with their start and end apart: 9, of which 9 were waited for; matrix products, arithmetic and copies ran while one was open for 2% of the time, Pallas kernels for 0%

commit v1 on v0

v1 whole, which is shorter than its diff:
```python
import functools
import math

import jax
import jax.numpy as jnp
from jax import lax
from jax.experimental import pallas as pl
from jax.experimental.pallas import tpu as pltpu
from jax.sharding import PartitionSpec as P

highest = lax.Precision.HIGHEST
high = lax.Precision.HIGH
ridge_weight = 0.1
decay_period = 128.0
lanes = 128


def split_three(x):
    a = lax.reduce_precision(x, 8, 7)
    b = lax.reduce_precision(x - a, 8, 7)
    c = x - a - b
    return [v.astype(jnp.bfloat16)[:, None] for v in (a, b, c)]


def left_form(rows):
    count, width = rows.shape
    norms = jnp.sum(jnp.square(rows.astype(jnp.float32)), axis=1) * (-1.0 / width)
    one = jnp.ones((count, 1), jnp.bfloat16)
    pad = jnp.zeros((count, lanes - width - 6), jnp.bfloat16)
    return jnp.concatenate(
        [rows * jnp.bfloat16(2.0 / width)] + split_three(norms) + [one, one, one, pad], axis=1
    )


def right_form(rows):
    count, width = rows.shape
    norms = jnp.sum(jnp.square(rows.astype(jnp.float32)), axis=1) * (-1.0 / width)
    one = jnp.ones((count, 1), jnp.bfloat16)
    pad = jnp.zeros((count, lanes - width - 6), jnp.bfloat16)
    return jnp.concatenate([rows, one, one, one] + split_three(norms) + [pad], axis=1)


def apply_body(tile, steps, a_ref, b_ref, v_ref, o_ref):
    total = None
    for j in range(steps):
        cols = slice(j * tile, (j + 1) * tile)
        logits = lax.dot_general(
            a_ref[...], b_ref[:, cols], (((1,), (0,)), ((), ())),
            preferred_element_type=jnp.float32,
        )
        part = jnp.dot(
            jnp.exp(logits).astype(jnp.bfloat16), v_ref[cols, :],
            preferred_element_type=jnp.float32,
        )
        total = part if total is None else total + part

    @pl.when(pl.program_id(1) == 0)
    def _():
        o_ref[...] = total

    @pl.when(pl.program_id(1) > 0)
    def _():
        o_ref[...] += total


def kernel_apply(a, b_t, v, tm=512, tk=1024, steps=2):
    m, n, labels = a.shape[0], b_t.shape[1], v.shape[1]
    tm = min(tm, m)
    tk = min(tk, n)
    while n % (tk * steps):
        steps -= 1
    span = tk * steps
    return pl.pallas_call(
        functools.partial(apply_body, tk, steps),
        out_shape=jax.ShapeDtypeStruct((m, labels), jnp.float32),
        grid=(m // tm, n // span),
        in_specs=[
            pl.BlockSpec((tm, lanes), lambda i, j: (i, 0)),
            pl.BlockSpec((lanes, span), lambda i, j: (0, j)),
            pl.BlockSpec((span, labels), lambda i, j: (j, 0)),
        ],
        out_specs=pl.BlockSpec((tm, labels), lambda i, j: (i, 0)),
        compiler_params=pltpu.CompilerParams(vmem_limit_bytes=40 * 1024 * 1024),
        cost_estimate=pl.CostEstimate(
            flops=2 * m * n * (lanes + labels) * 2,
            bytes_accessed=(m + n) * lanes * 2 + n * labels * 2 + m * labels * 4,
            transcendentals=m * n,
        ),
    )(a, b_t, v)


def body(points, centers, coeffs, targets, diag_inv, low_left, low_right, decay_rates, block_ranks):
    samp, ind = lax.axis_size("samp"), lax.axis_size("ind")
    samp_at, ind_at = lax.axis_index("samp"), lax.axis_index("ind")
    rows, width = points.shape
    inducing_rows, labels = coeffs.shape
    blocks, size, rank = low_left.shape
    chunks = 2
    chunk_rows = rows // chunks
    share = chunk_rows // ind
    own_count = inducing_rows // samp

    all_points = lax.all_gather(points, "samp", axis=0)
    point_left = left_form(points)
    center_right = right_form(centers).T

    residuals = []
    for c in range(chunks):
        part = kernel_apply(point_left[c * chunk_rows:(c + 1) * chunk_rows], center_right, coeffs)
        pred = lax.psum_scatter(part, "ind", scatter_dimension=0, tiled=True)
        own = lax.dynamic_slice_in_dim(targets, c * chunk_rows + ind_at * share, share, 0)
        resid = (jax.nn.sigmoid(pred) - own.astype(jnp.float32)).astype(jnp.bfloat16)
        residuals.append(lax.all_gather(resid, ("samp", "ind"), axis=0, tiled=True))

    own_centers = left_form(lax.dynamic_slice_in_dim(centers, samp_at * own_count, own_count, 0))
    point_right = [
        right_form(all_points[:, c * chunk_rows:(c + 1) * chunk_rows].reshape(-1, width)).T
        for c in range(chunks)
    ]

    mask = jnp.arange(rank)[None, :] < block_ranks[:, None]
    left = jnp.where(mask[:, None, :], low_left, 0).astype(jnp.float32)
    right = jnp.where(mask[:, None, :], low_right, 0).astype(jnp.float32)
    decays = jnp.exp(-decay_rates / decay_period)
    inv_left = jnp.einsum("kab,kbr->kar", diag_inv, left, precision=high)
    step_maps = decays[:, :, None] * jnp.eye(rank, dtype=jnp.float32) - jnp.einsum(
        "kar,kas->krs", right, inv_left, precision=high
    )
    eye = jnp.eye(rank, dtype=jnp.float32)
    current = jnp.pad(eye, ((0, 0), (0, blocks * rank)))
    maps = [current]
    for k in range(blocks):
        current = jnp.dot(step_maps[k], current, precision=high) + jnp.pad(
            eye, ((0, 0), ((k + 1) * rank, (blocks - 1 - k) * rank))
        )
        maps.append(current)
    state_maps = jnp.concatenate(maps[:-1], axis=0)
    exit_map = maps[-1][:, rank:]
    transfers = lax.all_gather(maps[-1][:, :rank], "ind", axis=0)
    entry = jnp.zeros((rank, ind * rank), jnp.float32)
    for d in range(ind - 1):
        moved = jnp.dot(transfers[d], entry, precision=high) + jnp.pad(
            eye, ((0, 0), (d * rank, (ind - 1 - d) * rank))
        )
        entry = jnp.where(d < ind_at, moved, entry)

    scaling = 1.0 / math.sqrt(rows * samp)
    first = kernel_apply(own_centers, point_right[0], residuals[0])
    half = own_count // 2
    gathered = []
    own_coeffs = lax.dynamic_slice_in_dim(coeffs, samp_at * own_count, own_count, 0)
    for h in range(2):
        rng = slice(h * half, (h + 1) * half)
        piece = first[rng] + kernel_apply(own_centers[rng], point_right[1], residuals[1])
        piece = piece * scaling + ridge_weight * own_coeffs[rng].astype(jnp.float32)
        gathered.append(lax.all_gather(piece, "samp", axis=0))
    gradient = jnp.concatenate(gathered, axis=1).reshape(blocks, size, labels)

    solved = jnp.einsum("kab,kbl->kal", diag_inv, gradient, precision=high)
    inputs = jnp.einsum("kar,kal->krl", right, solved, precision=high).reshape(blocks * rank, labels)
    offset = jnp.dot(exit_map, inputs, precision=high)
    offsets = lax.all_gather(offset, "ind", axis=0, tiled=True)
    local = jnp.dot(state_maps[:, rank:], inputs, precision=high)
    entering = jnp.dot(entry, offsets, precision=high)
    states = local + jnp.dot(state_maps[:, :rank], entering, precision=high)
    direction = solved - jnp.einsum(
        "kar,krl->kal", inv_left, states.reshape(blocks, rank, labels), precision=high
    )
    return direction.reshape(inducing_rows, labels)


def solution(mesh):
    return jax.shard_map(
        body,
        mesh=mesh,
        in_specs=(
            P("samp", None),
            P("ind", None),
            P("ind", None),
            P("samp", None),
            P("ind", None, None),
            P("ind", None, None),
            P("ind", None, None),
            P("ind", None),
            P("ind"),
        ),
        out_specs=P("ind", None),
        check_vma=False,
    )
```

time: 497 us -> 377 us (0.76)
  matrix products: 279 us -> 57.6 us
  Pallas kernels: 0 us -> 64.2 us
  local copies, waits for them, and re-layouts: 8.32 us -> 45.4 us
  starting transfers between devices: 26.6 us -> 0.96 us
  blocking collectives: 15 us -> 29.1 us
  waiting for transfers between devices: 132 us -> 141 us
    dot_general x159 -> x32, matrix products: 279 us -> 57.6 us  [the longest x16 15 us: body(): jnp.dot(step_maps[k], current, precision=high)]
    all_gather x0 -> x5, waiting for transfers between devices: none -> 98 us  [the longest x2 60.8 us: body(): residuals.append(lax.all_gather(resid, ('samp', 'ind'), axis=0, tiled=True))]
    psum x1 -> x0, waiting for transfers between devices: 91.3 us -> none  [body(): summed = lax.psum(pieces, 'samp')]
    pallas_call x0 -> x5, Pallas kernels: none -> 64.2 us  [kernel_apply(): pl.pallas_call(functools.partial(apply_body, tk, steps), out_shape=jax.Sh...]
    ppermute x7 -> x0, starting transfers between devices: 26.6 us -> none  [from_behind(): return lax.ppermute(block, axis, route)]
    concatenate x0 -> x6, local copies, waits for them, and re-layouts: none -> 20.3 us  [the longest x4 13.9 us: right_form(): jnp.concatenate([rows, one, one, one] + split_three(norms) + [pad], axis=1)]
    all_gather x1 -> x2, blocking collectives: 15 us -> 29.1 us  [the longest x1 14.6 us: body(): offsets = lax.all_gather(offset, 'ind', axis=0, tiled=True)]
    reduce_scatter x1 -> x2, waiting for transfers between devices: 35.1 us -> 42.8 us  [body(): pred = lax.psum_scatter(part, 'ind', scatter_dimension=0, tiled=True)]
  transfers between devices with their start and end apart: 9 -> 7, of which waited for: 9 -> 6; matrix products, arithmetic and copies ran while one was open for 2% -> 14% of each run, Pallas kernels for 0% -> 9%
where the time goes in v1:
time: 377 us; the launch traced here: 371 us
  waiting for transfers between devices  141 us (37%)
  Pallas kernels  64.2 us (17%)
  matrix products  57.6 us (15%)
  local copies, waits for them, and re-layouts  45.4 us (12%)
  blocking collectives  29.1 us (8%)
  other arithmetic  16.1 us (4%)
  between operations  15.9 us (4%)
    pallas_call x5, Pallas kernels, kernel_apply(): pl.pallas_call(functools.partial(apply_body, tk, steps), out_shape=jax.Sh...  64.2 us
    all_gather x2, waiting for transfers between devices, body(): residuals.append(lax.all_gather(resid, ('samp', 'ind'), axis=0, tiled=True))  60.8 us
    reduce_scatter x2, waiting for transfers between devices, body(): pred = lax.psum_scatter(part, 'ind', scatter_dimension=0, tiled=True)  42.8 us
    all_gather x2, waiting for transfers between devices, body(): gathered.append(lax.all_gather(piece, 'samp', axis=0))  37.2 us
    dot_general x16, matrix products, body(): jnp.dot(step_maps[k], current, precision=high)  15 us
    all_gather x1, blocking collectives, body(): offsets = lax.all_gather(offset, 'ind', axis=0, tiled=True)  14.6 us
    all_gather x1, blocking collectives, body(): transfers = lax.all_gather(maps[-1][:, :rank], 'ind', axis=0)  14.4 us
    dot_general x1, matrix products, body(): solved = jnp.einsum('kab,kbl->kal', diag_inv, gradient, precision=high)  14.2 us
  transfers between devices with their start and end apart: 7, of which 6 were waited for; matrix products, arithmetic and copies ran while one was open for 14% of the time, Pallas kernels for 9%

profile of v1, /device:TPU:0, one launch (start us, length us, event | category | flops | bytes accessed | tf_op | source)
XLA Modules:
  0.0 370.8 jit_solution(14801485622325592541)
XLA Ops:
  7.4 1.0 multiply_reduce_fusion.4
  8.8 1.2 copy.26
  10.4 1.1 copy.29
  12.3 1.2 fusion.13
  13.7 3.3 concatenate.26
  17.4 1.0 broadcast_in_dim.16
  18.5 10.1 %concatenate.28 = bf16[8192,128]{0,1:T(8,128)(2,1)S(1)} concatenate(bf16[8192,64]{0,1:T(8,128)(2,1)} %param.10, bf16[8192,3]{0,1:T(4,128)(2,1)S(1)} %concatenate.27, bf16[8192,1]{0,1:T(2,128)(2,1)S(1)} %get-tuple-element.23, bf16[8192,1]{0,1:T(2,128)(2,1)S(1)} %get-tuple-element.22, bf16[8192,1]{0,1:T(2,128)(2,1)S(1)} %get-tuple-element.21, bf16[8192,58]{0,1:T(8,128)(2,1)} %broadcast_in_dim.16), dimensions={1} | concatenate | bytes 4194304 | tf_op jit(solution)/shard_map/concatenate | solution.py:40
  28.6 1.6 copy-done.3
  30.2 16.5 %shard_map.91 = f32[1024,128]{1,0:T(8,128)} custom-call(bf16[1024,128]{1,0:T(8,128)(2,1)S(1)} %get-tuple-element.19.a_ref, bf16[128,8192]{1,0:T(8,128)(2,1)S(1)} %bitcast.145, bf16[8192,128]{1,0:T(8,128)(2,1)S(1)} %copy-done.3), custom_call_target="tpu_custom_call" | custom-call | flops 8589934592 | bytes 4980736 | tf_op jit(solution)/shard_map/pallas_call | solution.py:73
  46.7 1.6 copy-done.4
  48.3 16.4 %shard_map.93 = f32[1024,128]{1,0:T(8,128)} custom-call(bf16[1024,128]{1,0:T(8,128)(2,1)S(1)} %get-tuple-element.20.a_ref, bf16[128,8192]{1,0:T(8,128)(2,1)S(1)} %bitcast.146, bf16[8192,128]{1,0:T(8,128)(2,1)S(1)} %copy-done.4), custom_call_target="tpu_custom_call" | custom-call | flops 8589934592 | bytes 4980736 | tf_op jit(solution)/shard_map/pallas_call | solution.py:73
  67.4 1.3 copy.24
  69.1 11.4 %reduce-scatter.3.cloned.1.call-done = f32[128,128]{1,0:T(8,128)} async-done(((f32[1024,128]{1,0:T(8,128)}), f32[128,128]{1,0:T(8,128)}) %reduce-scatter.3.cloned.1.call-update) | async-done | bytes 65552 | tf_op jit(solution)/shard_map/reduce_scatter | solution.py:110
  80.4 31.5 %reduce-scatter.5.cloned.1.call-done = f32[128,128]{1,0:T(8,128)} async-done(((f32[1024,128]{1,0:T(8,128)}), f32[128,128]{1,0:T(8,128)}) %reduce-scatter.5.cloned.1.call-update) | async-done | bytes 65552 | tf_op jit(solution)/shard_map/reduce_scatter | solution.py:110
  111.9 1.6 subtract_convert_fusion.1
  114.9 2.4 fusion.12
  117.3 3.1 concatenate.24.a_ref
  121.3 12.4 %fusion.14 = f32[16,64,512]{2,1,0:T(8,128)} fusion(f32[16,512,512]{2,1,0:T(8,128)} %param.13, bf16[16,512,64]{1,2,0:T(8,128)(2,1)S(1)} %copy-done.13, pred[16,64]{1,0:T(8,128)(4,1)S(1)} %iota_compare_fusion.1), kind=kOutput, calls=%fused_computation.43 | convolution fusion | flops 1611137024 | bytes 19923968 | tf_op jit(solution)/shard_map/kab,kbr->kar/dot_general | solution.py:125
  134.0 1.8 reshape.254
  138.1 1.0 concatenate.29
  139.1 2.8 concatenate.25
  141.9 23.8 %all-gather.12.cloned.1.call-done.v_ref = bf16[4096,128]{1,0:T(8,128)(2,1)} async-done(((bf16[128,128]{1,0:T(8,128)(2,1)}), bf16[4096,128]{1,0:T(8,128)(2,1)}) %all-gather.12.cloned.1.call-update) | async-done | bytes 1048592 | tf_op jit(solution)/shard_map/all_gather | solution.py:113
  166.6 1.2 copy-done.5
  167.8 7.8 %shard_map.95 = f32[1024,128]{1,0:T(8,128)S(1)} custom-call(bf16[1024,128]{1,0:T(8,128)(2,1)S(1)} %copy-done.2, bf16[128,4096]{1,0:T(8,128)(2,1)S(1)} %bitcast.147, bf16[4096,128]{1,0:T(8,128)(2,1)S(1)} %copy-done.5), custom_call_target="tpu_custom_call" | custom-call | flops 4294967296 | bytes 2883584 | tf_op jit(solution)/shard_map/pallas_call | solution.py:73
  175.7 7.9 %shard_map.94 = f32[1024,128]{1,0:T(8,128)S(1)} custom-call(bf16[1024,128]{1,0:T(8,128)(2,1)S(1)} %get-tuple-element.15.a_ref, bf16[128,4096]{1,0:T(8,128)(2,1)S(1)} %bitcast.148, bf16[4096,128]{1,0:T(8,128)(2,1)S(1)} %copy-done.6), custom_call_target="tpu_custom_call" | custom-call | flops 4294967296 | bytes 2883584 | tf_op jit(solution)/shard_map/pallas_call | solution.py:73
  184.3 37.0 %all-gather.10.cloned.1.call-done.v_ref = bf16[4096,128]{1,0:T(8,128)(2,1)} async-done(((bf16[128,128]{1,0:T(8,128)(2,1)}), bf16[4096,128]{1,0:T(8,128)(2,1)}) %all-gather.10.cloned.1.call-update) | async-done | bytes 1048592 | tf_op jit(solution)/shard_map/all_gather | solution.py:113
  221.4 1.2 copy-done.7
  222.6 15.7 %shard_map.92 = f32[2048,128]{1,0:T(8,128)S(1)} custom-call(bf16[2048,128]{1,0:T(8,128)(2,1)S(1)} %concatenate.24.a_ref, bf16[128,4096]{1,0:T(8,128)(2,1)S(1)} %bitcast.149, bf16[4096,128]{1,0:T(8,128)(2,1)S(1)} %copy-done.7), custom_call_target="tpu_custom_call" | custom-call | flops 8589934592 | bytes 3670016 | tf_op jit(solution)/shard_map/pallas_call | solution.py:73
  238.3 2.3 fusion.23
  241.4 2.4 convolution_subtract_fusion
  244.8 1.0 constant_dynamic-update-slice_fusion.13
  248.7 1.0 constant_dynamic-update-slice_fusion.9
  249.7 1.0 constant_dynamic-update-slice_fusion.8
  250.7 1.0 constant_dynamic-update-slice_fusion.7
  251.7 1.0 constant_dynamic-update-slice_fusion.6
  255.6 1.0 constant_dynamic-update-slice_fusion.2
  256.6 1.0 constant_dynamic-update-slice_fusion.1
  257.6 1.0 constant_dynamic-update-slice_fusion
  258.9 14.4 %all-gather.3 = f32[512,64]{1,0:T(8,128)S(1)} all-gather(f32[64,64]{1,0:T(8,128)S(1)} %slice.181), channel_id=5, replica_groups=mesh['samp'=4,'ind'=8] {'ind'}, dimensions={0}, use_global_device_ids=true | all-gather | bytes 147456 | tf_op jit(solution)/shard_map/all_gather | solution.py:139
  274.8 37.0 %all-gather.18.cloned.1.call-done = f32[4096,128]{1,0:T(8,128)} async-done(((f32[1024,128]{1,0:T(8,128)}), f32[4096,128]{1,0:T(8,128)}) %all-gather.18.cloned.1.call-update) | async-done | bytes 2097168 | tf_op jit(solution)/shard_map/all_gather | solution.py:156
  311.9 4.5 %pad_maximum_fusion = f32[4,2048,128]{2,1,0:T(8,128)} fusion(f32[4,1024,128]{2,1,0:T(8,128)} %bitcast.158, f32[4,1024,128]{2,1,0:T(8,128)} %bitcast.157), kind=kLoop, calls=%fused_computation.2 | loop fusion | flops 1048576 | bytes 8388608 | tf_op jit(solution)/shard_map/concatenate | solution.py:157
  316.4 14.2 %fusion.52 = f32[16,128,512]{2,1,0:T(8,128)S(1)} fusion(f32[16,512,128]{2,1,0:T(8,128)} %bitcast.150, f32[16,512,512]{2,1,0:T(8,128)} %param.13), kind=kOutput, calls=%fused_computation.147 | convolution fusion | flops 3221225472 | bytes 25165824 | tf_op jit(solution)/shard_map/kab,kbl->kal/dot_general | solution.py:159
  330.6 1.6 fusion.17
  332.6 14.6 %all_gather.43 = f32[512,128]{1,0:T(8,128)S(1)} all-gather(f32[64,128]{1,0:T(8,128)S(1)} %fusion.28), channel_id=1, replica_groups=mesh['samp'=4,'ind'=8] {'ind'}, dimensions={0}, use_global_device_ids=true | all-gather | bytes 294912 | tf_op jit(solution)/shard_map/all_gather | solution.py:162
  347.5 1.4 fusion.18
  348.9 4.7 %fusion.2 = f32[1024,128]{1,0:T(8,128)S(1)} fusion(f32[1024,128]{1,0:T(8,128)S(1)} %fusion.18, f32[1024,128]{1,0:T(8,128)S(1)} %bitcast.152, f32[1024,1088]{1,0:T(8,128)} %get-tuple-element.62), kind=kOutput, calls=%fused_computation.25 | convolution fusion | flops 805437440 | bytes 5767168 | tf_op jit(solution)/shard_map/dot_general | solution.py:163
  353.6 4.0 %bitcast_subtract_fusion = f32[16,512,128]{1,2,0:T(8,128)} fusion(f32[16,128,512]{2,1,0:T(8,128)S(1)} %fusion.52, f32[16,64,512]{2,1,0:T(8,128)S(1)} %copy-done.8, f32[16,64,128]{2,1,0:T(8,128)S(1)} %bitcast.159), kind=kOutput, calls=%fused_computation.3 | convolution fusion | flops 403701760 | bytes 11010048 | tf_op jit(solution)/shard_map/kar,krl->kal/dot_general | solution.py:166
  357.6 5.3 %copy.32 = f32[16,512,128]{2,1,0:T(8,128)} copy(f32[16,512,128]{1,2,0:T(8,128)} %bitcast_subtract_fusion) | data formatting | bytes 8388608 | tf_op jit(solution)/shard_map/sub | solution.py:166
  (98 shorter events, 21.5 us)
Async XLA Ops:
  7.4 73.1 %reduce-scatter.3.cloned.1.call-start = ((), (), s32[]{:S(2)}) async-start(), calls=%async_computation.2 | async-start | bytes 589824 | tf_op jit(solution)/shard_map/reduce_scatter | solution.py:110
  12.3 4.7 %copy-start.9 = (bf16[8192,64]{0,1:T(8,128)(2,1)S(1)}, bf16[8192,64]{0,1:T(8,128)(2,1)}, u32[]{:S(2)}) copy-start(bf16[8192,64]{0,1:T(8,128)(2,1)} %param.10) | copy-start | bytes 3145732
  13.7 4.8 %copy-start.10 = (bf16[2048,58]{1,0:T(8,128)(2,1)}, bf16[2048,58]{1,0:T(8,128)(2,1)S(1)}, u32[]{:S(2)}) copy-start(bf16[2048,58]{1,0:T(8,128)(2,1)S(1)} %broadcast.175) | copy-start | bytes 712708
  28.6 1.6 copy-start.3
  46.6 65.3 %reduce-scatter.5.cloned.1.call-start = ((), (), s32[]{:S(2)}) async-start(), calls=%async_computation.4 | async-start | bytes 589824 | tf_op jit(solution)/shard_map/reduce_scatter | solution.py:110
  46.7 1.6 copy-start.4
  64.7 52.6 %copy-start.11 = (bf16[2048,58]{1,0:T(8,128)(2,1)S(1)}, bf16[2048,58]{1,0:T(8,128)(2,1)}, u32[]{:S(2)}) copy-start(bf16[2048,58]{1,0:T(8,128)(2,1)} %copy-done.10) | copy-start | bytes 712708
  64.8 69.2 %all-gather.14.cloned.1.call-start = ((), (), s32[]{:S(2)}) async-start(), calls=%async_computation.6 | async-start | bytes 1310720 | tf_op jit(solution)/shard_map/all_gather | solution.py:103
  65.3 100.3 %all-gather.12.cloned.1.call-start = ((), (), s32[]{:S(2)}) async-start(), calls=%async_computation.5 | async-start | bytes 1081344 | tf_op jit(solution)/shard_map/all_gather | solution.py:113
  67.4 53.1 %copy-start.15 = (s32[16]{0:T(128)S(1)}, s32[16]{0:T(128)}, u32[]{:S(2)}) copy-start(s32[16]{0:T(128)} %param.17) | copy-start | bytes 196
  113.5 107.9 %all-gather.10.cloned.1.call-start = ((), (), s32[]{:S(2)}) async-start(), calls=%async_computation.3 | async-start | bytes 1081344 | tf_op jit(solution)/shard_map/all_gather | solution.py:113
  117.3 4.0 %copy-start.13 = (bf16[16,512,64]{1,2,0:T(8,128)(2,1)S(1)}, bf16[16,512,64]{1,2,0:T(8,128)(2,1)}, u32[]{:S(2)}) copy-start(bf16[16,512,64]{1,2,0:T(8,128)(2,1)} %param.14) | copy-start | bytes 3145732
  133.7 141.1 %all-gather.16.cloned.1.call-start = ((), (), s32[]{:S(2)}) async-start(), calls=%async_computation.7 | async-start | bytes 2621440 | tf_op jit(solution)/shard_map/all_gather | solution.py:156
  165.6 0.9 copy-start.2
  166.6 1.2 copy-start.5
  167.8 7.9 %copy-start.6 = (bf16[4096,128]{1,0:T(8,128)(2,1)S(1)}, bf16[4096,128]{1,0:T(8,128)(2,1)}, u32[]{:S(2)}) copy-start(bf16[4096,128]{1,0:T(8,128)(2,1)} %all-gather.12.cloned.1.call-done.v_ref) | copy-start | bytes 3145732
  183.5 0.8 copy-start
  221.4 1.2 copy-start.7
  222.6 15.7 %copy-start.1 = (f32[1024,128]{1,0:T(8,128)S(1)}, f32[1024,128]{1,0:T(8,128)}, u32[]{:S(2)}) copy-start(f32[1024,128]{1,0:T(8,128)} %copy-done) | copy-start | bytes 1572868
  222.6 18.0 %copy-start.14 = (f32[16,64]{1,0:T(8,128)S(1)}, f32[16,64]{1,0:T(8,128)}, u32[]{:S(2)}) copy-start(f32[16,64]{1,0:T(8,128)} %param.16) | copy-start | bytes 12292
  238.3 3.2 copy-start.12
  240.6 71.3 %all-gather.18.cloned.1.call-start = ((), (), s32[]{:S(2)}) async-start(), calls=%async_computation.8 | async-start | bytes 2621440 | tf_op jit(solution)/shard_map/all_gather | solution.py:156
  332.3 21.3 %copy-start.8 = (f32[16,64,512]{2,1,0:T(8,128)S(1)}, f32[16,64,512]{2,1,0:T(8,128)}, u32[]{:S(2)}) copy-start(f32[16,64,512]{2,1,0:T(8,128)} %fusion.14) | copy-start | bytes 6291460
Sparse Core Ops, SparseCore 0:
  46.8 33.6 reduce-scatter.2
  82.8 29.0 reduce-scatter.4
Sparse Core Ops, SparseCore 1:
  67.1 29.1 all-gather.13
  113.6 52.0 all-gather.11
  168.5 52.8 all-gather.9
  240.7 34.1 all-gather.15
  276.7 35.1 all-gather.17

commit v2 on v1

--- a/solution.py
+++ b/solution.py
@@ -24,20 +24,71 @@
 
 def left_form(rows):
     count, width = rows.shape
-    norms = jnp.sum(jnp.square(rows.astype(jnp.float32)), axis=1) * (-1.0 / width)
-    one = jnp.ones((count, 1), jnp.bfloat16)
-    pad = jnp.zeros((count, lanes - width - 6), jnp.bfloat16)
-    return jnp.concatenate(
-        [rows * jnp.bfloat16(2.0 / width)] + split_three(norms) + [one, one, one, pad], axis=1
-    )
+    turned = rows.T
+    norms = jnp.sum(jnp.square(turned.astype(jnp.float32)), axis=0) * (-1.0 / width)
+    pieces = [v.T for v in split_three(norms)]
+    pad = jnp.zeros((lanes - width - 6, count), jnp.bfloat16)
+    one = jnp.ones((3, count), jnp.bfloat16)
+    return jnp.concatenate([turned * jnp.bfloat16(2.0 / width)] + pieces + [one, pad], axis=0).T
 
 
 def right_form(rows):
     count, width = rows.shape
-    norms = jnp.sum(jnp.square(rows.astype(jnp.float32)), axis=1) * (-1.0 / width)
-    one = jnp.ones((count, 1), jnp.bfloat16)
-    pad = jnp.zeros((count, lanes - width - 6), jnp.bfloat16)
-    return jnp.concatenate([rows, one, one, one] + split_three(norms) + [pad], axis=1)
+    turned = rows.T
+    norms = jnp.sum(jnp.square(turned.astype(jnp.float32)), axis=0) * (-1.0 / width)
+    pieces = [v.T for v in split_three(norms)]
+    pad = jnp.zeros((lanes - width - 6, count), jnp.bfloat16)
+    return jnp.concatenate([turned, jnp.ones((3, count), jnp.bfloat16)] + pieces + [pad], axis=0)
+
+
+def halves(x):
+    top = x.astype(jnp.bfloat16)
+    return top, (x - top.astype(jnp.float32)).astype(jnp.bfloat16)
+
+
+def solve_body(inv_ref, grad_ref, right_ref, solved_ref, input_ref):
+    inv_top, inv_low = halves(inv_ref[0])
+    grad_top, grad_low = halves(grad_ref[0])
+    dot = functools.partial(jnp.dot, preferred_element_type=jnp.float32)
+    solved = dot(inv_top, grad_low) + dot(inv_low, grad_top) + dot(inv_top, grad_top)
+    solved_ref[0] = solved
+    top, low = halves(solved)
+    right = right_ref[0]
+    input_ref[0] = dot(right, low) + dot(right, top)
+
+
+def block_solve(inv, grad, right_t):
+    blocks, size, labels = grad.shape
+    rank = right_t.shape[1]
+    spec = lambda *shape: pl.BlockSpec((1,) + shape, lambda k: (k, 0, 0))
+    return pl.pallas_call(
+        solve_body,
+        out_shape=(
+            jax.ShapeDtypeStruct((blocks, size, labels), jnp.float32),
+            jax.ShapeDtypeStruct((blocks, rank, labels), jnp.float32),
+        ),
+        grid=(blocks,),
+        in_specs=[spec(size, size), spec(size, labels), spec(rank, size)],
+        out_specs=(spec(size, labels), spec(rank, labels)),
+        compiler_params=pltpu.CompilerParams(vmem_limit_bytes=32 * 1024 * 1024),
+        cost_estimate=pl.CostEstimate(
+            flops=6 * blocks * size * labels * (size + rank),
+            bytes_accessed=blocks * size * (size + 2 * labels) * 4,
+            transcendentals=0,
+        ),
+    )(inv, grad, right_t)
+
+
+def partner(at, step, count):
+    return at ^ step if count & (count - 1) == 0 else (at + step) % count
+
+
+def exchange(block, axis):
+    count = lax.axis_size(axis)
+    return [block] + [
+        lax.ppermute(block, axis, [(partner(i, d, count), i) for i in range(count)])
+        for d in range(1, count)
+    ]
 
 
 def apply_body(tile, steps, a_ref, b_ref, v_ref, o_ref):
@@ -95,28 +146,14 @@
     rows, width = points.shape
     inducing_rows, labels = coeffs.shape
     blocks, size, rank = low_left.shape
-    chunks = 2
-    chunk_rows = rows // chunks
-    share = chunk_rows // ind
+    share = rows // ind
     own_count = inducing_rows // samp
 
-    all_points = lax.all_gather(points, "samp", axis=0)
-    point_left = left_form(points)
-    center_right = right_form(centers).T
-
-    residuals = []
-    for c in range(chunks):
-        part = kernel_apply(point_left[c * chunk_rows:(c + 1) * chunk_rows], center_right, coeffs)
-        pred = lax.psum_scatter(part, "ind", scatter_dimension=0, tiled=True)
-        own = lax.dynamic_slice_in_dim(targets, c * chunk_rows + ind_at * share, share, 0)
-        resid = (jax.nn.sigmoid(pred) - own.astype(jnp.float32)).astype(jnp.bfloat16)
-        residuals.append(lax.all_gather(resid, ("samp", "ind"), axis=0, tiled=True))
-
+    point_right = exchange(right_form(points), "samp")
+    part = kernel_apply(left_form(points), right_form(centers), coeffs)
+    pred = lax.psum_scatter(part, "ind", scatter_dimension=0, tiled=True)
+    own_targets = lax.dynamic_slice_in_dim(targets, ind_at * share, share, 0)
     own_centers = left_form(lax.dynamic_slice_in_dim(centers, samp_at * own_count, own_count, 0))
-    point_right = [
-        right_form(all_points[:, c * chunk_rows:(c + 1) * chunk_rows].reshape(-1, width)).T
-        for c in range(chunks)
-    ]
 
     mask = jnp.arange(rank)[None, :] < block_ranks[:, None]
     left = jnp.where(mask[:, None, :], low_left, 0).astype(jnp.float32)
@@ -126,6 +163,19 @@
     step_maps = decays[:, :, None] * jnp.eye(rank, dtype=jnp.float32) - jnp.einsum(
         "kar,kas->krs", right, inv_left, precision=high
     )
+    own_targets, step_maps = lax.optimization_barrier((own_targets, step_maps))
+
+    resid = (jax.nn.sigmoid(pred) - own_targets.astype(jnp.float32)).astype(jnp.bfloat16)
+    residual = lax.all_gather(resid, "ind", axis=0, tiled=True)
+    summed = None
+    for form, piece in zip(point_right, exchange(residual, "samp")):
+        term = kernel_apply(own_centers, form, piece)
+        summed = term if summed is None else summed + term
+    scaling = 1.0 / math.sqrt(rows * samp)
+    own_coeffs = lax.dynamic_slice_in_dim(coeffs, samp_at * own_count, own_count, 0)
+    own_gradient = summed * scaling + ridge_weight * own_coeffs.astype(jnp.float32)
+
+    own_gradient, step_maps = lax.optimization_barrier((own_gradient, step_maps))
     eye = jnp.eye(rank, dtype=jnp.float32)
     current = jnp.pad(eye, ((0, 0), (0, blocks * rank)))
     maps = [current]
@@ -144,20 +194,16 @@
         )
         entry = jnp.where(d < ind_at, moved, entry)
 
-    scaling = 1.0 / math.sqrt(rows * samp)
-    first = kernel_apply(own_centers, point_right[0], residuals[0])
-    half = own_count // 2
-    gathered = []
-    own_coeffs = lax.dynamic_slice_in_dim(coeffs, samp_at * own_count, own_count, 0)
-    for h in range(2):
-        rng = slice(h * half, (h + 1) * half)
-        piece = first[rng] + kernel_apply(own_centers[rng], point_right[1], residuals[1])
-        piece = piece * scaling + ridge_weight * own_coeffs[rng].astype(jnp.float32)
-        gathered.append(lax.all_gather(piece, "samp", axis=0))
-    gradient = jnp.concatenate(gathered, axis=1).reshape(blocks, size, labels)
-
-    solved = jnp.einsum("kab,kbl->kal", diag_inv, gradient, precision=high)
-    inputs = jnp.einsum("kar,kal->krl", right, solved, precision=high).reshape(blocks * rank, labels)
+    gradient = jnp.zeros((inducing_rows, labels), jnp.float32)
+    for d, piece in enumerate(exchange(own_gradient, "samp")):
+        gradient = lax.dynamic_update_slice_in_dim(
+            gradient, piece, partner(samp_at, d, samp) * own_count, 0
+        )
+    gradient = gradient.reshape(blocks, size, labels)
+
+    right_t = jnp.swapaxes(jnp.where(mask[:, None, :], low_right, 0), 1, 2)
+    solved, inputs = block_solve(diag_inv, gradient, right_t)
+    inputs = inputs.reshape(blocks * rank, labels)
     offset = jnp.dot(exit_map, inputs, precision=high)
     offsets = lax.all_gather(offset, "ind", axis=0, tiled=True)
     local = jnp.dot(state_maps[:, rank:], inputs, precision=high)

time: 377 us -> 256 us (0.68); the launches traced: 371 us -> 255 us
  waiting for transfers between devices: 141 us -> 36.4 us
  matrix products: 57.6 us -> 26.5 us
  Pallas kernels: 64.2 us -> 82.3 us
  local copies, waits for them, and re-layouts: 45.4 us -> 27.5 us
  blocking collectives: 29.1 us -> 43.9 us
  starting transfers between devices: 0.96 us -> 11.8 us
    all_gather x5 -> x0, waiting for transfers between devices: 98 us -> none  [the longest x2 60.8 us: body(): residuals.append(lax.all_gather(resid, ('samp', 'ind'), axis=0, tiled=True))]
    reduce_scatter x2 -> x1, waiting for transfers between devices: 42.8 us -> 5.22 us  [body(): pred = lax.psum_scatter(part, 'ind', scatter_dimension=0, tiled=True)]
    ppermute x0 -> x9, waiting for transfers between devices: none -> 31.2 us  [exchange(): lax.ppermute(block, axis, [(partner(i, d, count), i) for i in range(count)])]
    pallas_call x0 -> x1, Pallas kernels: none -> 17.5 us  [block_solve(): pl.pallas_call(solve_body, out_shape=(jax.ShapeDtypeStruct((blocks, size,...]
    dot_general x2 -> x0, matrix products: 15.9 us -> none  [the longest x1 14.2 us: body(): solved = jnp.einsum('kab,kbl->kal', diag_inv, gradient, precision=high)]
    all_gather x0 -> x1, blocking collectives: none -> 15.1 us  [body(): residual = lax.all_gather(resid, 'ind', axis=0, tiled=True)]
    ppermute x0 -> x9, starting transfers between devices: none -> 11.8 us  [exchange(): lax.ppermute(block, axis, [(partner(i, d, count), i) for i in range(count)])]
    dot_general x16, matrix products: 15 us -> 4.18 us  [body(): jnp.dot(step_maps[k], current, precision=high)]
  transfers between devices with their start and end apart: 7 -> 10, of which waited for: 6 -> 6; matrix products, arithmetic and copies ran while one was open for 14% -> 19% of each run, Pallas kernels for 9% -> 22%
where the time goes in v2:
time: 256 us; the launch traced here: 255 us
  Pallas kernels  82.3 us (32%)
  blocking collectives  43.9 us (17%)
  waiting for transfers between devices  36.4 us (14%)
  local copies, waits for them, and re-layouts  27.5 us (11%)
  matrix products  26.5 us (10%)
  between operations  14 us (5%)
  other arithmetic  12.5 us (5%)
  starting transfers between devices  11.8 us (5%)
    pallas_call x5, Pallas kernels, kernel_apply(): pl.pallas_call(functools.partial(apply_body, tk, steps), out_shape=jax.Sh...  64.9 us
    ppermute x9, waiting for transfers between devices, exchange(): lax.ppermute(block, axis, [(partner(i, d, count), i) for i in range(count)])  31.2 us
    pallas_call x1, Pallas kernels, block_solve(): pl.pallas_call(solve_body, out_shape=(jax.ShapeDtypeStruct((blocks, size,...  17.5 us
    all_gather x1, blocking collectives, body(): residual = lax.all_gather(resid, 'ind', axis=0, tiled=True)  15.1 us
    all_gather x1, blocking collectives, body(): transfers = lax.all_gather(maps[-1][:, :rank], 'ind', axis=0)  14.4 us
    all_gather x1, blocking collectives, body(): offsets = lax.all_gather(offset, 'ind', axis=0, tiled=True)  14.3 us
    ppermute x9, starting transfers between devices, exchange(): lax.ppermute(block, axis, [(partner(i, d, count), i) for i in range(count)])  11.8 us
    concatenate x2, local copies, waits for them, and re-layouts, right_form(): jnp.concatenate([turned, jnp.ones((3, count), jnp.bfloat16)] + pieces + [...  11.5 us
  transfers between devices with their start and end apart: 10, of which 6 were waited for; matrix products, arithmetic and copies ran while one was open for 19% of the time, Pallas kernels for 22%

profile of v2, /device:TPU:0, one launch (start us, length us, event | category | flops | bytes accessed | tf_op | source)
XLA Modules:
  0.0 254.9 jit_solution(16996829603108638299)
XLA Ops:
  6.5 1.1 multiply_reduce_fusion.2
  7.8 1.4 concatenate.16.b_ref
  9.2 4.0 %collective-permute-start.4 = (bf16[128,2048]{1,0:T(8,128)(2,1)S(1)}, bf16[128,2048]{1,0:T(8,128)(2,1)}, u32[]{:S(2)}, u32[]{:S(2)}) collective-permute-start(bf16[128,2048]{1,0:T(8,128)(2,1)S(1)} %concatenate.16.b_ref), channel_id=1, source_target_pairs={{24,0},{16,8},{8,16},{0,24},{25,1},{17,9},{9,17},{1,25},{26,2},{18... | collective-permute-start | bytes 1572872 | tf_op jit(solution)/shard_map/ppermute | solution.py:89
  13.2 0.5 collective-permute-start.2
  13.8 1.0 broadcast_multiply_fusion
  14.8 0.5 concatenate.17
  15.3 1.0 copy.26.a_ref
  16.7 1.0 broadcast_in_dim.41
  17.8 10.1 %concatenate.18.b_ref = bf16[128,8192]{1,0:T(8,128)(2,1)S(1)} concatenate(bf16[64,8192]{1,0:T(8,128)(2,1)} %bitcast.133, bf16[3,8192]{1,0:T(4,128)(2,1)S(1)} %broadcast_in_dim.40, bf16[1,8192]{1,0:T(2,128)(2,1)S(1)} %get-tuple-element.21, bf16[1,8192]{1,0:T(2,128)(2,1)S(1)} %get-tuple-element.20, bf16[1,8192]{1,0:T(2,128)(2,1)S(1)} %get-tuple-element.19, ...), dimensions={0} | concatenate | bytes 4194304 | tf_op jit(solution)/shard_map/concatenate | solution.py:41
  27.9 1.0 copy-done.3
  28.9 1.6 copy-done.4
  30.5 31.4 %shard_map.91 = f32[2048,128]{1,0:T(8,128)S(1)} custom-call(bf16[2048,128]{1,0:T(8,128)(2,1)S(1)} %copy-done.3, bf16[128,8192]{1,0:T(8,128)(2,1)S(1)} %concatenate.18.b_ref, bf16[8192,128]{1,0:T(8,128)(2,1)S(1)} %copy-done.4), custom_call_target="tpu_custom_call" | custom-call | flops 17179869184 | bytes 5767168 | tf_op jit(solution)/shard_map/pallas_call | solution.py:124
  61.9 1.0 copy-done.2
  62.8 1.0 constant_dynamic-slice_fusion.1
  64.5 0.4 copy-done.8
  65.0 11.4 %fusion.13 = f32[16,64,512]{2,1,0:T(8,128)S(1)} fusion(f32[16,512,512]{2,1,0:T(8,128)} %inv_ref.1, bf16[16,512,64]{1,2,0:T(8,128)(2,1)} %param.14, pred[16,64]{1,0:T(8,128)(4,1)S(1)} %iota_compare_fusion.1), kind=kOutput, calls=%fused_computation.39 | convolution fusion | flops 1611137024 | bytes 19923968 | tf_op jit(solution)/shard_map/kab,kbr->kar/dot_general | solution.py:162
  76.5 1.6 copy.21
  78.1 1.1 copy.23
  79.2 1.4 copy.22
  80.6 2.9 %convolution_subtract_fusion = f32[16,64,64]{2,1,0:T(8,128)} fusion(f32[16,64,512]{2,1,0:T(8,128)S(1)} %fusion.13, bf16[16,512,64]{1,2,0:T(8,128)(2,1)} %param.15, pred[16,64]{1,0:T(8,128)(4,1)S(1)} %iota_compare_fusion.1, f32[64,64]{1,0:T(8,128)S(1)} %fusion.65, f32[16,64]{1,0:T(8,128)S(1)} %multiply_exponential_fusion), kind=kOutput, calls=%fused_computation.22 | convolution fusion | flops 201981952 | bytes 3429376 | tf_op jit(solution)/shard_map/kar,kas->krs/dot_general | solution.py:163
  83.4 1.9 multiply_bitcast_fusion
  85.3 2.7 %fusion.12 = (bf16[1,2048]{0,1:T(8,128)(2,1)}, bf16[1,2048]{0,1:T(8,128)(2,1)}) fusion(f32[1,2048]{0,1:T(8,128)} %copy.21, f32[1,2048]{0,1:T(8,128)} %copy.22), kind=kLoop, calls=%fused_computation.37 | loop fusion | flops 10240 | bytes 24576 | tf_op jit(solution)/shard_map/convert_element_type | solution.py:22
  88.2 3.2 %concatenate.15 = bf16[128,2048]{0,1:T(8,128)(2,1)S(1)} concatenate(bf16[64,2048]{0,1:T(8,128)(2,1)} %multiply_bitcast_fusion, bf16[1,2048]{0,1:T(8,128)(2,1)} %copy.23, bf16[1,2048]{0,1:T(8,128)(2,1)} %get-tuple-element.18, bf16[1,2048]{0,1:T(8,128)(2,1)} %get-tuple-element.17, bf16[3,2048]{0,1:T(8,128)(2,1)S(1)} %broadcast.130.clone, bf16[58,2048]{0,1:T(8,128)(2,1)S(1)} %broadcast.131.clone), dimensions={0} | concatenate | bytes 1048576 | tf_op jit(solution)/shard_map/concatenate | solution.py:32
  91.6 5.2 %reduce-scatter.2.cloned.1.call-done = f32[256,128]{1,0:T(8,128)} async-done(((f32[2048,128]{1,0:T(8,128)}), f32[256,128]{1,0:T(8,128)}) %reduce-scatter.2.cloned.1.call-update) | async-done | bytes 131088 | tf_op jit(solution)/shard_map/reduce_scatter | solution.py:154
  96.8 0.9 subtract_convert_fusion
  97.8 15.1 %all_gather.12.v_ref = bf16[2048,128]{1,0:T(8,128)(2,1)S(1)} all-gather(bf16[256,128]{1,0:T(8,128)(2,1)S(1)} %subtract_convert_fusion), channel_id=1, replica_groups=mesh['samp'=4,'ind'=8] {'ind'}, dimensions={0}, use_global_device_ids=true | all-gather | bytes 589824 | tf_op jit(solution)/shard_map/all_gather | solution.py:169
  112.9 2.4 collective-permute-start.5
  115.3 0.8 collective-permute-start.3
  116.1 7.6 %shard_map.92 = f32[2048,128]{1,0:T(8,128)S(1)} custom-call(bf16[2048,128]{1,0:T(8,128)(2,1)S(1)} %bitcast.129, bf16[128,2048]{1,0:T(8,128)(2,1)S(1)} %concatenate.16.b_ref, bf16[2048,128]{1,0:T(8,128)(2,1)S(1)} %all_gather.12.v_ref), custom_call_target="tpu_custom_call" | custom-call | flops 4294967296 | bytes 2621440 | tf_op jit(solution)/shard_map/pallas_call | solution.py:124
  123.7 0.5 collective-permute-start.1
  124.2 4.4 %collective-permute-done.5.v_ref = bf16[2048,128]{1,0:T(8,128)(2,1)S(1)} collective-permute-done((bf16[2048,128]{1,0:T(8,128)(2,1)S(1)}, bf16[2048,128]{1,0:T(8,128)(2,1)S(1)}, u32[]{:S(2)}, u32[]{:S(2)}) %collective-permute-start.5) | collective-permute-done | bytes 524320 | tf_op jit(solution)/shard_map/ppermute | solution.py:89
  128.6 8.6 %shard_map.95 = f32[2048,128]{1,0:T(8,128)S(1)} custom-call(bf16[2048,128]{1,0:T(8,128)(2,1)S(1)} %bitcast.130, bf16[128,2048]{1,0:T(8,128)(2,1)} %collective-permute-done.4.b_ref, bf16[2048,128]{1,0:T(8,128)(2,1)S(1)} %collective-permute-done.5.v_ref), custom_call_target="tpu_custom_call" | custom-call | flops 4294967296 | bytes 2621440 | tf_op jit(solution)/shard_map/pallas_call | solution.py:124
  137.3 2.0 collective-permute-done.3.v_ref
  139.2 8.6 %shard_map.94 = f32[2048,128]{1,0:T(8,128)S(1)} custom-call(bf16[2048,128]{1,0:T(8,128)(2,1)S(1)} %bitcast.131, bf16[128,2048]{1,0:T(8,128)(2,1)} %collective-permute-done.2.b_ref, bf16[2048,128]{1,0:T(8,128)(2,1)S(1)} %collective-permute-done.3.v_ref), custom_call_target="tpu_custom_call" | custom-call | flops 4294967296 | bytes 2621440 | tf_op jit(solution)/shard_map/pallas_call | solution.py:124
  147.9 8.6 %shard_map.93 = f32[2048,128]{1,0:T(8,128)S(1)} custom-call(bf16[2048,128]{1,0:T(8,128)(2,1)S(1)} %bitcast.132, bf16[128,2048]{1,0:T(8,128)(2,1)} %collective-permute-done.b_ref, bf16[2048,128]{1,0:T(8,128)(2,1)S(1)} %collective-permute-done.1.v_ref), custom_call_target="tpu_custom_call" | custom-call | flops 4294967296 | bytes 2621440 | tf_op jit(solution)/shard_map/pallas_call | solution.py:124
  156.6 1.3 multiply_add_fusion
  157.9 1.7 collective-permute-start.6
  159.6 0.9 collective-permute-start.7
  160.5 1.0 collective-permute-start.8
  165.8 14.4 %all-gather = f32[512,64]{1,0:T(8,128)S(1)} all-gather(f32[64,64]{1,0:T(8,128)S(1)} %slice.117), channel_id=2, replica_groups=mesh['samp'=4,'ind'=8] {'ind'}, dimensions={0}, use_global_device_ids=true | all-gather | bytes 147456 | tf_op jit(solution)/shard_map/all_gather | solution.py:189
  182.0 2.1 collective-permute-done.6
  184.1 21.0 %collective-permute-done.7 = f32[2048,128]{1,0:T(8,128)S(1)} collective-permute-done((f32[2048,128]{1,0:T(8,128)S(1)}, f32[2048,128]{1,0:T(8,128)S(1)}, u32[]{:S(2)}, u32[]{:S(2)}) %collective-permute-start.7) | collective-permute-done | bytes 1048608 | tf_op jit(solution)/shard_map/ppermute | solution.py:89
  205.1 1.7 collective-permute-done.8
  206.9 17.5 %shard_map.96 = (f32[16,512,128]{2,1,0:T(8,128)S(1)}, f32[16,64,128]{2,1,0:T(8,128)S(1)}) custom-call(f32[16,512,512]{2,1,0:T(8,128)} %inv_ref.1, f32[16,512,128]{2,1,0:T(8,128)S(1)} %bitcast.126, bf16[16,64,512]{2,1,0:T(8,128)(2,1)S(1)} %fusion.16.right_ref), custom_call_target="tpu_custom_call" | custom-call | flops 3623878656 | bytes 25165824 | tf_op jit(solution)/shard_map/pallas_call | solution.py:64
  224.8 14.3 %all_gather.15 = f32[512,128]{1,0:T(8,128)S(1)} all-gather(f32[64,128]{1,0:T(8,128)S(1)} %fusion.22), channel_id=1, replica_groups=mesh['samp'=4,'ind'=8] {'ind'}, dimensions={0}, use_global_device_ids=true | all-gather | bytes 294912 | tf_op jit(solution)/shard_map/all_gather | solution.py:208
  239.7 2.4 fusion.2
  242.1 3.4 %fusion.73 = f32[16,512,128]{2,1,0:T(8,128)S(1)} fusion(f32[16,64,512]{2,1,0:T(8,128)S(1)} %copy-done.6, f32[16,64,128]{2,1,0:T(8,128)S(1)} %bitcast.136), kind=kOutput, calls=%fused_computation.142 | convolution fusion | flops 402653184 | bytes 6815744 | tf_op jit(solution)/shard_map/kar,krl->kal/dot_general | solution.py:212
  245.5 2.5 sub.95
  (81 shorter events, 8.7 us)
Async XLA Ops:
  6.5 74.0 %copy-start = (bf16[2048,128]{1,0:T(8,128)(2,1)S(1)}, bf16[2048,128]{1,0:T(8,128)(2,1)}, u32[]{:S(2)}) copy-start(bf16[2048,128]{1,0:T(8,128)(2,1)} %param.12) | copy-start | bytes 1572868
  6.5 9.8 %copy-start.7 = (bf16[8192,64]{0,1:T(8,128)(2,1)S(1)}, bf16[8192,64]{0,1:T(8,128)(2,1)}, u32[]{:S(2)}) copy-start(bf16[8192,64]{0,1:T(8,128)(2,1)} %param.10) | copy-start | bytes 3145732
  6.5 90.3 %reduce-scatter.2.cloned.1.call-start = ((), (), s32[]{:S(2)}) async-start(), calls=%async_computation.1 | async-start | bytes 1179648 | tf_op jit(solution)/shard_map/reduce_scatter | solution.py:154
  9.2 114.5 %collective-permute-start.4 = (bf16[128,2048]{1,0:T(8,128)(2,1)S(1)}, bf16[128,2048]{1,0:T(8,128)(2,1)}, u32[]{:S(2)}, u32[]{:S(2)}) collective-permute-start(bf16[128,2048]{1,0:T(8,128)(2,1)S(1)} %concatenate.16.b_ref), channel_id=1, source_target_pairs={{24,0},{16,8},{8,16},{0,24},{25,1},{17,9},{9,17},{1,25},{26,2},{18... | collective-permute-start | bytes 1572872 | tf_op jit(solution)/shard_map/ppermute | solution.py:89
  13.2 124.1 %collective-permute-start.2 = (bf16[128,2048]{1,0:T(8,128)(2,1)S(1)}, bf16[128,2048]{1,0:T(8,128)(2,1)}, u32[]{:S(2)}, u32[]{:S(2)}) collective-permute-start(bf16[128,2048]{1,0:T(8,128)(2,1)S(1)} %concatenate.16.b_ref), channel_id=1, source_target_pairs={{16,0},{24,8},{0,16},{8,24},{17,1},{25,9},{1,17},{9,25},{18,2},{26... | collective-permute-start | bytes 1572872 | tf_op jit(solution)/shard_map/ppermute | solution.py:89
  13.7 134.2 %collective-permute-start = (bf16[128,2048]{1,0:T(8,128)(2,1)S(1)}, bf16[128,2048]{1,0:T(8,128)(2,1)}, u32[]{:S(2)}, u32[]{:S(2)}) collective-permute-start(bf16[128,2048]{1,0:T(8,128)(2,1)S(1)} %concatenate.16.b_ref), channel_id=1, source_target_pairs={{8,0},{0,8},{24,16},{16,24},{9,1},{1,9},{25,17},{17,25},{10,2},{2,... | collective-permute-start | bytes 1572872 | tf_op jit(solution)/shard_map/ppermute | solution.py:89
  27.8 1.0 copy-start.3
  28.9 1.6 copy-start.4
  30.5 34.4 %copy-start.12 = (s32[16]{0:T(128)S(1)}, s32[16]{0:T(128)}, u32[]{:S(2)}) copy-start(s32[16]{0:T(128)} %param.17) | copy-start | bytes 196
  61.8 1.0 copy-start.2
  64.1 0.8 copy-start.8
  65.0 15.6 %copy-start.11 = (f32[16,64]{1,0:T(8,128)S(1)}, f32[16,64]{1,0:T(8,128)}, u32[]{:S(2)}) copy-start(f32[16,64]{1,0:T(8,128)} %param.16) | copy-start | bytes 12292
  76.4 11.6 %copy-start.5 = (f32[16,64,512]{2,1,0:T(8,128)}, f32[16,64,512]{2,1,0:T(8,128)S(1)}, u32[]{:S(2)}) copy-start(f32[16,64,512]{2,1,0:T(8,128)S(1)} %fusion.13) | copy-start | bytes 6291460
  88.0 3.4 %copy-start.9 = (bf16[16,512,64]{1,2,0:T(8,128)(2,1)S(1)}, bf16[16,512,64]{1,2,0:T(8,128)(2,1)}, u32[]{:S(2)}) copy-start(bf16[16,512,64]{1,2,0:T(8,128)(2,1)} %param.15) | copy-start | bytes 3145732
  112.9 15.7 %collective-permute-start.5 = (bf16[2048,128]{1,0:T(8,128)(2,1)S(1)}, bf16[2048,128]{1,0:T(8,128)(2,1)S(1)}, u32[]{:S(2)}, u32[]{:S(2)}) collective-permute-start(bf16[2048,128]{1,0:T(8,128)(2,1)S(1)} %all_gather.12.v_ref), channel_id=1, source_target_pairs={{24,0},{16,8},{8,16},{0,24},{25,1},{17,9},{9,17},{1,25},{26,2},{18... | collective-permute-start | bytes 1572872 | tf_op jit(solution)/shard_map/ppermute | solution.py:89
  115.3 23.9 %collective-permute-start.3 = (bf16[2048,128]{1,0:T(8,128)(2,1)S(1)}, bf16[2048,128]{1,0:T(8,128)(2,1)S(1)}, u32[]{:S(2)}, u32[]{:S(2)}) collective-permute-start(bf16[2048,128]{1,0:T(8,128)(2,1)S(1)} %all_gather.12.v_ref), channel_id=1, source_target_pairs={{16,0},{24,8},{0,16},{8,24},{17,1},{25,9},{1,17},{9,25},{18,2},{26... | collective-permute-start | bytes 1572872 | tf_op jit(solution)/shard_map/ppermute | solution.py:89
  123.7 24.2 %collective-permute-start.1 = (bf16[2048,128]{1,0:T(8,128)(2,1)S(1)}, bf16[2048,128]{1,0:T(8,128)(2,1)S(1)}, u32[]{:S(2)}, u32[]{:S(2)}) collective-permute-start(bf16[2048,128]{1,0:T(8,128)(2,1)S(1)} %all_gather.12.v_ref), channel_id=1, source_target_pairs={{8,0},{0,8},{24,16},{16,24},{9,1},{1,9},{25,17},{17,25},{10,2},{2,... | collective-permute-start | bytes 1572872 | tf_op jit(solution)/shard_map/ppermute | solution.py:89
  156.6 4.9 %copy-start.10 = (f32[16,64,64]{2,1,0:T(8,128)S(1)}, f32[16,64,64]{2,1,0:T(8,128)}, u32[]{:S(2)}) copy-start(f32[16,64,64]{2,1,0:T(8,128)} %convolution_subtract_fusion) | copy-start | bytes 786436
  157.9 26.1 %collective-permute-start.6 = (f32[2048,128]{1,0:T(8,128)S(1)}, f32[2048,128]{1,0:T(8,128)S(1)}, u32[]{:S(2)}, u32[]{:S(2)}) collective-permute-start(f32[2048,128]{1,0:T(8,128)S(1)} %multiply_add_fusion), channel_id=1, source_target_pairs={{8,0},{0,8},{24,16},{16,24},{9,1},{1,9},{25,17},{17,25},{10,2},{2,... | collective-permute-start | bytes 3145736 | tf_op jit(solution)/shard_map/ppermute | solution.py:89
  159.6 45.5 %collective-permute-start.7 = (f32[2048,128]{1,0:T(8,128)S(1)}, f32[2048,128]{1,0:T(8,128)S(1)}, u32[]{:S(2)}, u32[]{:S(2)}) collective-permute-start(f32[2048,128]{1,0:T(8,128)S(1)} %multiply_add_fusion), channel_id=1, source_target_pairs={{16,0},{24,8},{0,16},{8,24},{17,1},{25,9},{1,17},{9,25},{18,2},{26... | collective-permute-start | bytes 3145736 | tf_op jit(solution)/shard_map/ppermute | solution.py:89
  160.5 46.3 %collective-permute-start.8 = (f32[2048,128]{1,0:T(8,128)S(1)}, f32[2048,128]{1,0:T(8,128)S(1)}, u32[]{:S(2)}, u32[]{:S(2)}) collective-permute-start(f32[2048,128]{1,0:T(8,128)S(1)} %multiply_add_fusion), channel_id=1, source_target_pairs={{24,0},{16,8},{8,16},{0,24},{25,1},{17,9},{9,17},{1,25},{26,2},{18... | collective-permute-start | bytes 3145736 | tf_op jit(solution)/shard_map/ppermute | solution.py:89
  224.4 17.6 %copy-start.6 = (f32[16,64,512]{2,1,0:T(8,128)S(1)}, f32[16,64,512]{2,1,0:T(8,128)}, u32[]{:S(2)}) copy-start(f32[16,64,512]{2,1,0:T(8,128)} %copy-done.5) | copy-start | bytes 6291460
  245.5 2.5 copy-start.1
Sparse Core Ops, SparseCore 0:
  63.0 33.8 reduce-scatter.1
